TPU v7x, 32 devices: a whole 2x2x4 slice. The times are simulated.
32 devices in a mesh: parts: 2 (over y), dp: 4 (over z), tensor: 2 (over x), seq: 2 (over core).
Axes of the slice: x: 2, y: 2, z: 4, core: 2. Of those that a mesh axis runs over, the one named last changes fastest.
Arguments:
- acts: bfloat16 [8192, 8192], P(('parts', 'dp', 'seq'), 'tensor'), parts along dimension 0, may hold values from -6 to 6
- grads: bfloat16 [8192, 32768], P(('parts', 'dp', 'seq'), 'tensor'), parts along dimension 0, may hold values from -0.029907227 to 0.029907227
- eig_in: bfloat16 [8192, 512], P('tensor'), may hold values from -0.0625 to 0.0625
- eig_out: bfloat16 [32768, 256], P('tensor'), may hold values from -0.03125 to 0.03125
- query_acts: bfloat16 [4096, 8192], P(('parts', 'dp', 'seq'), 'tensor'), parts along dimension 0, may hold values from -6 to 6
- query_grads: bfloat16 [4096, 32768], P(('parts', 'dp', 'seq'), 'tensor'), parts along dimension 0, may hold values from -0.029907227 to 0.029907227
- eigenvalues: float32 [256, 512], P('tensor'), may hold values from 0.05 to 5
- lengths: int32 [8, 16], P(('parts', 'dp')), parts along dimension 0, may hold values from 1 to 256, 1024 in all within a row
- owner: int32 [8, 16, 1], P(('parts', 'dp')), parts along dimension 0, may hold values from 0 to 3; in each aligned block of 16 rows (0 to 15, 16 to 31, ..., all dimensions but the last counted through in order) at most 4 rows name the same one
Outputs:
- doc_scores: float32 [128, 64], P(('parts', 'dp'), ('tensor', 'seq')), parts along dimension 0
There are 2 independent parts, one for each index of `parts`. A program takes and returns all parts, laid end to end along the dimension named above; an argument that names none is the same for every part. Nothing has to cross between parts.
Inputs may be any that keep to these rules, and one draw needn't show every extreme that they name: `lengths`: each row gives, in order, the token counts of the 16 documents of one packed sequence; a row sums to 1024. The documents of one sequence name any one owner at most 4 times; in some sequences an owner is named exactly 4 times.
All inputs are finite; a program needn't handle non-finite values.
Results may differ from a plain program's by a relative error of at most 0.0065.
Values may be sent and summed in bfloat16 or wider, within the bound.
A program may use at most 128 MiB of HBM per device.

v0:
```python
import jax
import jax.numpy as jnp
from jax import lax
from jax.sharding import PartitionSpec as P

QTOK = 32


damping = 0.01


def damp_queries(out_rows, in_rows, eigenvalues):
    item_count = out_rows.shape[0] // QTOK
    out_blocks = out_rows.reshape(item_count, QTOK, out_rows.shape[1])
    in_blocks = in_rows.reshape(item_count, QTOK, in_rows.shape[1])
    outer_sum = jnp.einsum(
        "qui,quj->qij", out_blocks, in_blocks, preferred_element_type=jnp.float32
    )
    return (outer_sum / (eigenvalues + damping)).astype(jnp.bfloat16)


def token_terms(in_rot, out_rot, damped):
    item_count = damped.shape[0]
    row_width = damped.shape[1]
    spread = lax.dot_general(
        in_rot,
        damped.reshape(item_count * row_width, damped.shape[2]),
        (((1,), (1,)), ((), ())),
        preferred_element_type=jnp.float32,
    )
    spread = spread.reshape(in_rot.shape[0], item_count, row_width)
    return jnp.einsum("tqi,ti->tq", spread, out_rot.astype(jnp.float32))


def per_device(acts, grads, eig_in, eig_out, query_acts, query_grads, eigenvalues, lengths, owner):
    highest = lax.Precision.HIGHEST
    tok_count = acts.shape[0]
    in_part = jnp.dot(acts, eig_in, preferred_element_type=jnp.float32)
    query_in_part = jnp.dot(query_acts, eig_in, preferred_element_type=jnp.float32)
    in_sum, query_in_sum = lax.psum((in_part, query_in_part), "tensor")
    in_rot = in_sum.astype(jnp.bfloat16)
    query_in = query_in_sum.astype(jnp.bfloat16)
    out_part = jnp.dot(grads, eig_out, preferred_element_type=jnp.float32)
    query_out_part = jnp.dot(query_grads, eig_out, preferred_element_type=jnp.float32)
    out_sum, query_out_sum = (
        lax.psum_scatter(out_part, "tensor", scatter_dimension=1, tiled=True),
        lax.psum_scatter(query_out_part, "tensor", scatter_dimension=1, tiled=True),
    )
    out_rot = out_sum.astype(jnp.bfloat16)
    query_out = query_out_sum.astype(jnp.bfloat16)
    damped = damp_queries(query_out, query_in, eigenvalues)
    scores = token_terms(in_rot, out_rot, lax.all_gather(damped, ("dp", "seq"), axis=0, tiled=True))
    doc_lengths = lengths[0]
    doc_ends = jnp.cumsum(doc_lengths)
    doc_begins = doc_ends - doc_lengths
    positions = lax.axis_index("seq") * tok_count + jnp.arange(tok_count, dtype=jnp.int32)
    member = (
        (positions[:, None] >= doc_begins[None, :]) & (positions[:, None] < doc_ends[None, :])
    ).astype(jnp.float32)
    doc_part = lax.dot_general(
        member,
        scores,
        (((0,), (0,)), ((), ())),
        precision=highest,
        preferred_element_type=jnp.float32,
    )
    owner_count = lax.axis_size("dp")
    doc_count = doc_lengths.shape[0]
    capacity = max(3, (doc_count + owner_count - 1) // owner_count)
    doc_owner = owner[0, :, 0]
    doc_order = jnp.arange(doc_count, dtype=jnp.int32)
    earlier = (
        (doc_owner[None, :] == doc_owner[:, None]) & (doc_order[None, :] < doc_order[:, None])
    ).astype(jnp.int32)
    doc_slot = jnp.sum(earlier, axis=1)
    target = doc_owner * capacity + doc_slot
    slot_rows = jnp.arange(owner_count * capacity, dtype=jnp.int32)
    placing = (slot_rows[:, None] == target[None, :]).astype(jnp.float32)
    shares = lax.psum_scatter(doc_part, ("tensor", "seq"), scatter_dimension=1, tiled=True)
    placed = jnp.dot(placing, shares, precision=highest, preferred_element_type=jnp.float32)
    owned_table = lax.all_to_all(
        placed.reshape(owner_count, capacity, shares.shape[1]),
        "dp",
        split_axis=0,
        concat_axis=0,
        tiled=True,
    )
    return owned_table.reshape(owner_count * capacity, owned_table.shape[2])


def solution(mesh):
    return jax.shard_map(
        per_device,
        mesh=mesh,
        in_specs=(
            P(("parts", "dp", "seq"), "tensor"),
            P(("parts", "dp", "seq"), "tensor"),
            P("tensor", None),
            P("tensor", None),
            P(("parts", "dp", "seq"), "tensor"),
            P(("parts", "dp", "seq"), "tensor"),
            P("tensor", None),
            P(("parts", "dp"), None),
            P(("parts", "dp"), None, None),
        ),
        out_specs=P(("parts", "dp"), ("tensor", "seq")),
        check_vma=False,
    )
```

profile of v0, /device:TPU:0, one launch (start us, length us, event | category | flops | bytes accessed | tf_op | source)
XLA Modules:
  0.0 218.1 jit_solution(5652053273264848939)
XLA Ops:
  6.5 0.0 copy-start
  6.5 0.0 reduce-scatter.6.cloned.1.call-start
  6.5 8.9 %fusion.18 = f32[256,256]{1,0:T(8,128)} fusion(bf16[256,16384]{1,0:T(8,128)(2,1)} %param.14, bf16[16384,256]{1,0:T(8,128)(2,1)} %param.12), kind=kOutput, calls=%fused_computation.28 | convolution fusion | flops 2147483648 | bytes 17039360 | tf_op jit(solution)/shard_map/dot_general | solution.py:44
  15.5 0.0 reduce-scatter.6.cloned.1.call-update
  15.5 0.0 reduce-scatter.8.cloned.1.call-start
  15.6 13.4 %fusion.20 = f32[512,256]{1,0:T(8,128)} fusion(bf16[512,16384]{1,0:T(8,128)(2,1)} %param.10, bf16[16384,256]{1,0:T(8,128)(2,1)} %param.12), kind=kOutput, calls=%fused_computation.30 | convolution fusion | flops 4294967296 | bytes 25690112 | tf_op jit(solution)/shard_map/dot_general | solution.py:43
  29.0 0.0 reduce-scatter.8.cloned.1.call-update
  29.0 0.0 copy-start.1
  29.0 0.0 all-gather.2.cloned.1.call-start
  29.1 0.0 copy-start.3
  29.1 5.9 %fusion.17 = f32[512,512]{1,0:T(8,128)S(1)} fusion(bf16[512,4096]{1,0:T(8,128)(2,1)} %param.9, bf16[4096,512]{1,0:T(8,128)(2,1)} %param.11), kind=kOutput, calls=%fused_computation.27 | convolution fusion | flops 2147483648 | bytes 9437184 | tf_op jit(solution)/shard_map/dot_general | solution.py:38
  35.0 0.0 copy-done
  35.0 0.0 copy-done.3
  35.1 0.0 copy-start.2
  35.1 0.0 copy-start.5
  35.1 2.0 fusion.19
  37.1 0.0 copy-done.1
  37.1 0.7 broadcast_add_fusion
  37.9 43.9 %all-reduce.2 = (bf16[256,512]{1,0:T(8,128)(2,1)S(1)}, bf16[512,512]{1,0:T(8,128)(2,1)}) all-reduce(f32[256,512]{1,0:T(8,128)} %fusion.19, f32[512,512]{1,0:T(8,128)S(1)} %fusion.17), channel_id=1, replica_groups=mesh['parts'=2,'dp'=4,'tensor'=2,'seq'=2] {'tensor'}, use_global_device_ids=true, to_apply=%region_4.0 | all-reduce | flops 393216 | bytes 2359296 | tf_op jit(solution)/shard_map/psum | solution.py:40
  81.8 0.0 copy-start.4
  81.8 0.0 reduce-scatter.6.cloned.1.call-done
  81.8 1.0 convert_element_type.23
  82.8 2.5 %divide_convert_fusion = bf16[8,128,512]{2,1,0:T(8,128)(2,1)} fusion(bf16[8,32,128]{2,1,0:T(8,128)(2,1)S(1)} %bitcast.38, bf16[8,32,512]{2,1,0:T(8,128)(2,1)S(1)} %bitcast.42, f32[128,512]{1,0:T(8,128)} %broadcast_add_fusion), kind=kOutput, calls=%fused_computation.2 | convolution fusion | flops 34603008 | bytes 1638400 | tf_op jit(solution)/shard_map/qui,quj->qij/dot_general | solution.py:16
  85.3 0.0 all-gather.2.cloned.1.call-update
  85.3 0.2 reduce-scatter.10.cloned.1.call-start
  85.5 0.0 copy-done.2
  85.5 0.1 copy.14
  85.6 0.1 reduce
  85.8 0.0 copy-done.5
  85.8 0.2 convert_reduce_fusion
  86.0 0.0 reduce-scatter.8.cloned.1.call-done
  86.0 1.0 convert_bitcast_fusion
  87.0 82.0 %all-gather.2.cloned.1.call-done = bf16[64,128,512]{2,1,0:T(8,128)(2,1)} async-done(((bf16[8,128,512]{2,1,0:T(8,128)(2,1)}), bf16[64,128,512]{2,1,0:T(8,128)(2,1)}) %all-gather.2.cloned.1.call-update) | async-done | bytes 8388624 | tf_op jit(solution)/shard_map/all_gather | solution.py:52
  169.0 0.0 copy-done.4
  169.0 7.1 %fusion.2 = bf16[512,64,128]{2,0,1:T(8,128)(2,1)S(1)} fusion(bf16[64,128,512]{2,1,0:T(8,128)(2,1)} %all-gather.2.cloned.1.call-done, bf16[512,512]{1,0:T(8,128)(2,1)S(1)} %copy-done.4), kind=kOutput, calls=%fused_computation.4 | convolution fusion | flops 4294967296 | bytes 17301504 | tf_op jit(solution)/shard_map/dot_general | solution.py:25
  176.0 5.1 %fusion = f32[512,1,64]{2,1,0:T(1,128)S(1)} fusion(bf16[512,64,128]{2,0,1:T(8,128)(2,1)S(1)} %fusion.2, bf16[512,128,1]{1,0,2:T(8,128)(2,1)S(1)} %convert_bitcast_fusion), kind=kOutput, calls=%fused_computation | convolution fusion | flops 8388608 | bytes 8650752 | tf_op jit(solution)/shard_map/tqi,ti->tq/dot_general | solution.py:32
  181.1 1.0 convolution_bitcast_fusion
  182.1 0.0 reduce-scatter.10.cloned.1.call-update
  182.2 18.0 %reduce-scatter.10.cloned.1.call-done = f32[16,16]{1,0:T(8,128)} async-done(((f32[64,16]{1,0:T(8,128)}), f32[16,16]{1,0:T(8,128)}) %reduce-scatter.10.cloned.1.call-update) | async-done | bytes 1040
  200.2 0.8 fusion.12
  201.0 10.0 %all_to_all.5 = f32[4,4,16]{2,1,0:T(4,128)S(1)} all-to-all(f32[4,4,16]{2,1,0:T(4,128)S(1)} %bitcast.39), channel_id=1, replica_groups=mesh['parts'=2,'dp'=4,'tensor'=2,'seq'=2] {'dp'}, dimensions={0} | all-to-all | bytes 2048 | tf_op jit(solution)/shard_map/all_to_all | solution.py:81
  211.0 0.6 copy.29
  (4 shorter events, 0.0 us)
Async XLA Ops:
  6.5 28.5 %copy-start = (bf16[256,4096]{1,0:T(8,128)(2,1)S(1)}, bf16[256,4096]{1,0:T(8,128)(2,1)}, u32[]{:S(2)}) copy-start(bf16[256,4096]{1,0:T(8,128)(2,1)} %param.13) | copy-start | bytes 6291460
  6.5 75.2 %reduce-scatter.6.cloned.1.call-start = ((), (), s32[]{:S(2)}) async-start(), calls=%async_computation.4 | async-start | bytes 393216 | tf_op jit(solution)/shard_map/reduce_scatter | solution.py:47
  15.5 70.5 %reduce-scatter.8.cloned.1.call-start = ((), (), s32[]{:S(2)}) async-start(), calls=%async_computation.6 | async-start | bytes 786432 | tf_op jit(solution)/shard_map/reduce_scatter | solution.py:46
  29.0 8.1 %copy-start.1 = (f32[128,512]{1,0:T(8,128)S(1)}, f32[128,512]{1,0:T(8,128)}, u32[]{:S(2)}) copy-start(f32[128,512]{1,0:T(8,128)} %param.15) | copy-start | bytes 786436
  29.0 139.9 %all-gather.2.cloned.1.call-start = ((), (), s32[]{:S(2)}) async-start(), calls=%async_computation.5 | async-start | bytes 9437184 | tf_op jit(solution)/shard_map/all_gather | solution.py:52
  29.1 6.0 %copy-start.3 = (bf16[4096,512]{1,0:T(8,128)(2,1)S(1)}, bf16[4096,512]{1,0:T(8,128)(2,1)}, u32[]{:S(2)}) copy-start(bf16[4096,512]{1,0:T(8,128)(2,1)} %param.11) | copy-start | bytes 12582916
  35.1 50.5 %copy-start.2 = (s32[1,16]{1,0:T(1,128)S(1)}, s32[1,16]{1,0:T(1,128)}, u32[]{:S(2)}) copy-start(s32[1,16]{1,0:T(1,128)} %param.16) | copy-start | bytes 196
  35.1 50.7 %copy-start.5 = (s32[1,16,1]{1,2,0:T(1,128)S(1)}, s32[1,16,1]{1,2,0:T(1,128)}, u32[]{:S(2)}) copy-start(s32[1,16,1]{1,2,0:T(1,128)} %param.17) | copy-start | bytes 196
  81.8 87.2 %copy-start.4 = (bf16[512,512]{1,0:T(8,128)(2,1)S(1)}, bf16[512,512]{1,0:T(8,128)(2,1)}, u32[]{:S(2)}) copy-start(bf16[512,512]{1,0:T(8,128)(2,1)} %get-tuple-element.6) | copy-start | bytes 1572868
  85.3 114.9 %reduce-scatter.10.cloned.1.call-start = ((), (), s32[]{:S(2)}) async-start(), calls=%async_computation.7 | async-start | bytes 40960
Sparse Core Ops, SparseCore 0:
  15.6 14.3 reduce-scatter.5
  32.4 16.2 reduce-scatter.7
  85.4 83.5 all-gather.1
  182.3 17.8 reduce-scatter.9
where the time goes:
time: 218 us
  waiting for transfers between devices  100 us (46%)
  blocking collectives  53.9 us (25%)
  matrix products  46.8 us (21%)
  between operations  13.2 us (6%)
  other arithmetic  3.02 us (1%)
    all_gather x1, waiting for transfers between devices, per_device(): lax.all_gather(damped, ('dp', 'seq'), axis=0, tiled=True)  82 us
    psum x1, blocking collectives, per_device(): in_sum, query_in_sum = lax.psum((in_part, query_in_part), 'tensor')  43.9 us
    unnamed x5, waiting for transfers between devices  18.1 us
    dot_general x1, matrix products, per_device(): out_part = jnp.dot(grads, eig_out, preferred_element_type=jnp.float32)  13.4 us
    all_to_all x1, blocking collectives, per_device(): lax.all_to_all(placed.reshape(owner_count, capacity, shares.shape[1]), 'd...  9.98 us
    dot_general x1, matrix products, per_device(): jnp.dot(query_grads, eig_out, preferred_element_type=jnp.float32)  8.94 us
    dot_general x1, matrix products, token_terms(): lax.dot_general(in_rot, damped.reshape(item_count * row_width, damped.sha...  7.05 us
    dot_general x1, matrix products, per_device(): in_part = jnp.dot(acts, eig_in, preferred_element_type=jnp.float32)  5.95 us
  transfers between devices with their start and end apart: 4, of which 2 were waited for; matrix products, arithmetic and copies ran while one was open for 12% of the time, Pallas kernels for 0%

commit v1 on v0

v1 whole, which is shorter than its diff:
```python
import functools

import jax
import jax.numpy as jnp
from jax import lax
from jax.experimental import pallas as pl
from jax.experimental.pallas import tpu as pltpu
from jax.sharding import PartitionSpec as P

QTOK = 32
PAD = 8
LANES = 128
GROUP = 16


damping = 0.01
MESH = pl.DeviceIdType.MESH
f32, bf16 = jnp.float32, jnp.bfloat16


def dot(a, b, dims=((1,), (0,)), precision=None):
    return lax.dot_general(a, b, (dims, ((), ())), precision=precision, preferred_element_type=f32)


def kernel(
    sizes, len_ref, own_ref, acts, grads, eig_in, eig_out, query_acts, query_grads, eigenvalues, out_ref,
    v_a, v_g, v_ei, v_eo, v_qa, v_qg,
    acc_ti, acc_to, acc_qi, acc_qo,
    send_ti, send_to, send_qi, send_qo,
    got_ti, got_to, got_qi, got_qo,
    tok_in, tok_out, que_in, que_out,
    levels, doc_grad, que_grad, pair, placed, table,
    load_sem, x_send, x_recv, core_send, core_recv, z_send, z_recv, last_send, last_recv,
):
    nz, nx, n_in, n_out, in_step, out_step, doc_count, capacity = sizes
    part, z, x, s = (lax.axis_index(name) for name in ("parts", "dp", "tensor", "seq"))
    n_all = nz * nx * 2
    me = (z * nx + x) * 2 + s
    rows, wide = acc_ti.shape[1:]
    ks = acc_to.shape[1]
    q_rows = acc_qo.shape[0]
    q_each = q_rows // QTOK
    q_all = nz * q_each

    def place(index):
        return lax.div(index, 2 * nx), lax.rem(lax.div(index, 2), nx), lax.rem(index, 2)

    def load(kind, c):
        src, dst = {
            "eo": lambda: (eig_out.at[pl.ds(c * out_step, out_step), :], v_eo.at[c]),
            "qg": lambda: (query_grads.at[:, pl.ds(c * out_step, out_step)], v_qg.at[c]),
            "g": lambda: (grads.at[:, pl.ds(c * out_step, out_step)], v_g.at[c]),
            "ei": lambda: (eig_in.at[pl.ds(c * in_step, in_step), :], v_ei.at[c]),
            "qa": lambda: (query_acts.at[:, pl.ds(c * in_step, in_step)], v_qa.at[c]),
            "a": lambda: (acts.at[:, pl.ds(c * in_step, in_step)], v_a.at[c]),
        }[kind]()
        row = ("eo", "qg", "g", "ei", "qa", "a").index(kind)
        return pltpu.make_async_copy(src, dst, load_sem.at[row, c])

    for c in range(n_out):
        load("eo", c).start()
        load("qg", c).start()
    for c in range(n_in):
        load("ei", c).start()
        load("qa", c).start()
    for c in range(n_out):
        load("g", c).start()
    for c in range(n_in):
        load("a", c).start()
    own_level = pltpu.make_async_copy(
        eigenvalues.at[:, pl.ds(pl.multiple_of(x * wide, LANES), wide)], levels.at[x], load_sem.at[6, 0]
    )
    own_level.start()

    barrier = pltpu.get_barrier_semaphore()

    def greet(r, carry):
        oz, ox, os = place(lax.rem(me + r, n_all))
        pl.semaphore_signal(barrier, inc=1, device_id=(part, oz, ox, os), device_id_type=MESH)
        return carry

    lax.fori_loop(1, n_all, greet, 0)

    def along_x(kind, r, arriving=False):
        other = lax.rem(x + r, nx)
        back = lax.rem(x + nx - r, nx)
        src, dst = {
            "ev": lambda: (eigenvalues.at[:, pl.ds(pl.multiple_of(other * wide, LANES), wide)], levels),
            "qi": lambda: (send_qi.at[other], got_qi),
            "qo": lambda: (send_qo, got_qo),
            "ti": lambda: (send_ti.at[other], got_ti),
            "to": lambda: (send_to, got_to),
        }[kind]()
        row = ("ev", "qi", "qo", "ti", "to").index(kind)

        def copy(slot):
            return pltpu.make_async_remote_copy(
                src_ref=src, dst_ref=dst.at[slot], send_sem=x_send.at[row, r], recv_sem=x_recv.at[row, r],
                device_id=(part, z, other, s), device_id_type=MESH,
            )

        return copy(back if arriving else x)

    def start_x(kind):
        for r in range(1, nx):
            along_x(kind, r).start()

    def wait_x(kind):
        for r in range(1, nx):
            along_x(kind, r, True).wait_recv()

    def summed(own, got):
        total = own
        for r in range(1, nx):
            total = total + got[lax.rem(x + nx - r, nx)].astype(f32)
        return total

    def rotate_out(kind, held, acc):
        acc[...] = jnp.zeros_like(acc)

        def step(c, carry):
            if kind == "qg":
                load("eo", c).wait()
            load(kind, c).wait()
            acc[...] += dot(held[c], v_eo[c])
            return carry

        lax.fori_loop(0, n_out, step, 0)

    def rotate_in(kind, held, acc):
        acc[...] = jnp.zeros_like(acc)

        def step(c, carry):
            if kind == "qa":
                load("ei", c).wait()
            load(kind, c).wait()
            for j in range(nx):
                acc[j] += dot(held[c], v_ei[c, :, j * wide:(j + 1) * wide])
            return carry

        lax.fori_loop(0, n_in, step, 0)

    rotate_out("qg", v_qg, acc_qo)
    send_qo[...] = acc_qo[...].astype(bf16)
    pl.semaphore_wait(barrier, n_all - 1)
    start_x("ev")
    start_x("qo")
    rotate_in("qa", v_qa, acc_qi)
    send_qi[...] = acc_qi[...].astype(bf16)
    start_x("qi")

    rotate_out("g", v_g, acc_to)
    send_to[...] = acc_to[...].astype(bf16)
    start_x("to")

    def along_z(kind, r, arriving=False):
        ref = que_out if kind == 0 else que_in
        other = lax.rem(z + r, nz)
        back = lax.rem(z + nz - r, nz)

        def copy(slot):
            return pltpu.make_async_remote_copy(
                src_ref=ref.at[slot], dst_ref=ref.at[slot], send_sem=z_send.at[kind, r], recv_sem=z_recv.at[kind, r],
                device_id=(part, other, x, s), device_id_type=MESH,
            )

        return copy(back if arriving else z)

    wait_x("qo")
    que_out[z] = summed(acc_qo[...], got_qo).T.astype(bf16)
    wait_x("qi")
    que_in[z] = summed(acc_qi[x], got_qi).astype(bf16)

    def start_z(r, carry):
        along_z(0, r).start()
        along_z(1, r).start()
        return carry

    lax.fori_loop(1, nz, start_z, 0)

    rotate_in("a", v_a, acc_ti)
    send_ti[...] = acc_ti[...].astype(bf16)
    start_x("ti")

    own_level.wait()
    wait_x("ev")
    levels[...] = 1.0 / (levels[...] + damping)

    def damp(zb):
        lane = lax.broadcasted_iota(jnp.int32, (1, q_rows), 1)
        scale = levels[...].reshape(ks, wide)

        def one(k, carry):
            keep = ((lane >= k * QTOK) & (lane < (k + 1) * QTOK)).astype(f32).astype(bf16)
            outer = dot(que_out[zb] * keep, que_in[zb])
            que_grad[:, zb * q_each + k] = (outer * scale).astype(bf16).reshape(ks // GROUP, GROUP, wide)
            return carry

        lax.fori_loop(0, q_each, one, 0)

    damp(z)

    def to_core(kind, slot):
        ref = tok_out if kind == 0 else tok_in
        return pltpu.make_async_remote_copy(
            src_ref=ref.at[slot], dst_ref=ref.at[slot], send_sem=core_send.at[kind], recv_sem=core_recv.at[kind],
            device_id=(part, z, x, 1 - s), device_id_type=MESH,
        )

    wait_x("to")
    tok_out[s] = summed(acc_to[...], got_to).T.astype(bf16)
    to_core(0, s).start()
    wait_x("ti")
    tok_in[s] = summed(acc_ti[x], got_ti).astype(bf16)
    to_core(1, s).start()
    to_core(0, 1 - s).wait_recv()
    to_core(1, 1 - s).wait_recv()

    def document(d, begin):
        end = begin + len_ref[0, d]
        total = None
        for half in range(2):
            at = lax.broadcasted_iota(jnp.int32, (1, rows), 1) + half * rows
            keep = ((at >= begin) & (at < end)).astype(f32).astype(bf16)
            term = dot(tok_out[half] * keep, tok_in[half])
            total = term if total is None else total + term
        doc_grad[:, d] = total.astype(bf16).reshape(ks // GROUP, GROUP, wide)
        return end

    lax.fori_loop(0, doc_count, document, jnp.int32(0))

    def damp_far(r, carry):
        along_z(0, r, True).wait_recv()
        along_z(1, r, True).wait_recv()
        damp(lax.rem(z + nz - r, nz))
        return carry

    lax.fori_loop(1, nz, damp_far, 0)

    pair[...] = jnp.zeros_like(pair)

    def pairs(g, carry):
        left = doc_grad[g].reshape(doc_count * GROUP, wide)
        right = que_grad[g].reshape(q_all * GROUP, wide)
        pair[...] += dot(left, right, ((1,), (1,)))
        return carry

    lax.fori_loop(0, ks // GROUP, pairs, 0)
    row = lax.broadcasted_iota(jnp.int32, pair.shape, 0)
    col = lax.broadcasted_iota(jnp.int32, pair.shape, 1)
    same = jnp.where(lax.rem(row, GROUP) == lax.rem(col, GROUP), pair[...], 0.0)
    by_doc = jnp.sum(same.reshape(doc_count, GROUP, q_all * GROUP), axis=1)
    fold_row = lax.broadcasted_iota(jnp.int32, (q_all * GROUP, LANES), 0)
    fold_col = lax.broadcasted_iota(jnp.int32, (q_all * GROUP, LANES), 1)
    fold = (lax.div(fold_row, GROUP) == fold_col).astype(f32)
    highest = lax.Precision.HIGHEST
    scores = dot(by_doc, fold, precision=highest)

    slot_row = lax.broadcasted_iota(jnp.int32, (nz * PAD, doc_count), 0)
    slot_col = lax.broadcasted_iota(jnp.int32, (nz * PAD, doc_count), 1)
    placing = jnp.zeros((nz * PAD, doc_count), f32)
    for d in range(doc_count):
        owner = own_ref[0, d]
        slot = jnp.int32(0)
        for e in range(d):
            slot = slot + jnp.where(own_ref[0, e] == owner, 1, 0)
        placing = jnp.where((slot_row == owner * PAD + slot) & (slot_col == d), 1.0, placing)
    placed[...] = dot(placing, scores, precision=highest).reshape(nz, PAD, LANES)

    def to_owner(r):
        oz, ox, os = place(lax.rem(me + r, n_all))
        return pltpu.make_async_remote_copy(
            src_ref=placed.at[oz], dst_ref=table.at[x * 2 + s, z], send_sem=last_send.at[r], recv_sem=last_recv.at[r],
            device_id=(part, oz, ox, os), device_id_type=MESH,
        )

    def from_source(r):
        oz, ox, os = place(lax.rem(me + n_all - r, n_all))
        return pltpu.make_async_remote_copy(
            src_ref=placed.at[0], dst_ref=table.at[ox * 2 + os, oz], send_sem=last_send.at[r], recv_sem=last_recv.at[r],
            device_id=(part, oz, ox, os), device_id_type=MESH,
        )

    def start_last(r, carry):
        to_owner(r).start()
        return carry

    lax.fori_loop(1, n_all, start_last, 0)
    table[x * 2 + s, z] = placed[z]

    for kind in ("ev", "qi", "qo", "ti", "to"):
        for r in range(1, nx):
            along_x(kind, r).wait_send()
    to_core(0, s).wait_send()
    to_core(1, s).wait_send()

    def sent_z(r, carry):
        along_z(0, r).wait_send()
        along_z(1, r).wait_send()
        return carry

    lax.fori_loop(1, nz, sent_z, 0)

    def finish_last(r, carry):
        from_source(r).wait_recv()
        to_owner(r).wait_send()
        return carry

    lax.fori_loop(1, n_all, finish_last, 0)

    width = out_ref.shape[1]
    block = x * 2 + s
    result = jnp.zeros((nz * PAD, width), f32)
    pick_row = lax.broadcasted_iota(jnp.int32, (LANES, width), 0)
    pick_col = lax.broadcasted_iota(jnp.int32, (LANES, width), 1)
    for side in range(2):
        total = table[side].reshape(nz * PAD, LANES)
        for ox in range(1, nx):
            total = total + table[ox * 2 + side].reshape(nz * PAD, LANES)
        query = lax.div(pick_row, q_each) * (2 * q_each) + side * q_each + lax.rem(pick_row, q_each)
        pick = ((query == block * width + pick_col) & (pick_row < q_all)).astype(f32)
        result = result + dot(total, pick, precision=highest)
    for zz in range(nz):
        out_ref[zz * capacity:(zz + 1) * capacity, :] = result[zz * PAD:zz * PAD + capacity, :]


def chunk(extent, most):
    return min(extent, most)


def per_device(acts, grads, eig_in, eig_out, query_acts, query_grads, eigenvalues, lengths, owner):
    nz, nx = lax.axis_size("dp"), lax.axis_size("tensor")
    rows, q_rows = acts.shape[0], query_acts.shape[0]
    ka, ks = eig_in.shape[1], eig_out.shape[1]
    wide = ka // nx
    in_step, out_step = chunk(acts.shape[1], 2048), chunk(grads.shape[1], 2048)
    n_in, n_out = acts.shape[1] // in_step, grads.shape[1] // out_step
    doc_count = lengths.shape[1]
    capacity = max(3, (doc_count + nz - 1) // nz)
    q_each = q_rows // QTOK
    q_all = nz * q_each
    n_all = nz * nx * 2
    width = q_all * 2 // (nx * 2)
    sizes = (nz, nx, n_in, n_out, in_step, out_step, doc_count, capacity)
    any_spec = pl.BlockSpec(memory_space=pl.ANY)
    smem = pl.BlockSpec(memory_space=pltpu.SMEM)
    dma = pltpu.SemaphoreType.DMA
    return pl.pallas_call(
        functools.partial(kernel, sizes),
        out_shape=jax.ShapeDtypeStruct((nz * capacity, width), f32),
        in_specs=[smem, smem] + [any_spec] * 7,
        out_specs=pl.BlockSpec(memory_space=pltpu.VMEM),
        scratch_shapes=[
            pltpu.VMEM((n_in, rows, in_step), bf16),
            pltpu.VMEM((n_out, rows, out_step), bf16),
            pltpu.VMEM((n_in, in_step, ka), bf16),
            pltpu.VMEM((n_out, out_step, ks), bf16),
            pltpu.VMEM((n_in, q_rows, in_step), bf16),
            pltpu.VMEM((n_out, q_rows, out_step), bf16),
            pltpu.VMEM((nx, rows, wide), f32),
            pltpu.VMEM((rows, ks), f32),
            pltpu.VMEM((nx, q_rows, wide), f32),
            pltpu.VMEM((q_rows, ks), f32),
            pltpu.VMEM((nx, rows, wide), bf16),
            pltpu.VMEM((rows, ks), bf16),
            pltpu.VMEM((nx, q_rows, wide), bf16),
            pltpu.VMEM((q_rows, ks), bf16),
            pltpu.VMEM((nx, rows, wide), bf16),
            pltpu.VMEM((nx, rows, ks), bf16),
            pltpu.VMEM((nx, q_rows, wide), bf16),
            pltpu.VMEM((nx, q_rows, ks), bf16),
            pltpu.VMEM((2, rows, wide), bf16),
            pltpu.VMEM((2, ks, rows), bf16),
            pltpu.VMEM((nz, q_rows, wide), bf16),
            pltpu.VMEM((nz, ks, q_rows), bf16),
            pltpu.VMEM((nx, ks // nx, wide), f32),
            pltpu.VMEM((ks // GROUP, doc_count, GROUP, wide), bf16),
            pltpu.VMEM((ks // GROUP, q_all, GROUP, wide), bf16),
            pltpu.VMEM((doc_count * GROUP, q_all * GROUP), f32),
            pltpu.VMEM((nz, PAD, LANES), f32),
            pltpu.VMEM((nx * 2, nz, PAD, LANES), f32),
            dma((7, max(n_in, n_out))),
            dma((5, nx)),
            dma((5, nx)),
            dma((2,)),
            dma((2,)),
            dma((2, nz)),
            dma((2, nz)),
            dma((n_all,)),
            dma((n_all,)),
        ],
        compiler_params=pltpu.CompilerParams(
            collective_id=0, has_side_effects=True, vmem_limit_bytes=63 * 1024 * 1024
        ),
        cost_estimate=pl.CostEstimate(
            flops=2 * (rows + q_rows) * (acts.shape[1] * ka + grads.shape[1] * ks),
            bytes_accessed=2 * (rows + q_rows) * (acts.shape[1] + grads.shape[1]),
            transcendentals=0,
        ),
    )(
        lengths, owner.reshape(1, doc_count), acts, grads, eig_in, eig_out, query_acts, query_grads, eigenvalues
    )


def solution(mesh):
    return jax.shard_map(
        per_device,
        mesh=mesh,
        in_specs=(
            P(("parts", "dp", "seq"), "tensor"),
            P(("parts", "dp", "seq"), "tensor"),
            P("tensor", None),
            P("tensor", None),
            P(("parts", "dp", "seq"), "tensor"),
            P(("parts", "dp", "seq"), "tensor"),
            P("tensor", None),
            P(("parts", "dp"), None),
            P(("parts", "dp"), None, None),
        ),
        out_specs=P(("parts", "dp"), ("tensor", "seq")),
        check_vma=False,
    )
```

time: 218 us -> 58.7 us (0.27)
  waiting for transfers between devices: 100 us -> 0 us
  Pallas kernels: 0 us -> 57.2 us
  blocking collectives: 53.9 us -> 0 us
  matrix products: 46.8 us -> 0 us
  between operations: 13.2 us -> 0.01 us
  other arithmetic: 3.02 us -> 0 us
    all_gather x1 -> x0, waiting for transfers between devices: 82 us -> none  [per_device(): lax.all_gather(damped, ('dp', 'seq'), axis=0, tiled=True)]
    pallas_call x0 -> x1, Pallas kernels: none -> 57.2 us  [per_device(): pl.pallas_call(functools.partial(kernel, sizes), out_shape=jax.ShapeDtype...]
    dot_general x8 -> x0, matrix products: 45.8 us -> none  [the longest x1 13.4 us: per_device(): out_part = jnp.dot(grads, eig_out, preferred_element_type=jnp.float32)]
    psum x1 -> x0, blocking collectives: 43.9 us -> none  [per_device(): in_sum, query_in_sum = lax.psum((in_part, query_in_part), 'tensor')]
    unnamed x5 -> x0, waiting for transfers between devices: 18.1 us -> none
    all_to_all x1 -> x0, blocking collectives: 9.98 us -> none  [per_device(): lax.all_to_all(placed.reshape(owner_count, capacity, shares.shape[1]), 'd...]
  transfers between devices with their start and end apart: 4 -> 0, of which waited for: 2 -> 0; matrix products, arithmetic and copies ran while one was open for 12% -> 0% of each run, Pallas kernels for 0% -> 0%
where the time goes in v1:
time: 58.7 us; the launch traced here: 58.5 us
  Pallas kernels  57.2 us (97%)
  local copies, waits for them, and re-layouts  1.3 us (2%)
    pallas_call x1, Pallas kernels, per_device(): pl.pallas_call(functools.partial(kernel, sizes), out_shape=jax.ShapeDtype...  57.2 us
    unnamed x1, local copies, waits for them, and re-layouts  1.3 us

profile of v1, /device:TPU:0, one launch (start us, length us, event | category | flops | bytes accessed | tf_op | source)
XLA Modules:
  0.0 58.5 jit_solution(9778372003707004190)
XLA Ops:
  0.0 57.2 %shard_map.91 = f32[16,16]{1,0:T(8,128)} custom-call(s32[1,16]{1,0:T(1,128)} %len_ref.1, s32[1,16]{1,0:T(1,128)} %bitcast.1, bf16[512,4096]{1,0:T(8,128)(2,1)} %acts.1, bf16[512,16384]{1,0:T(8,128)(2,1)} %grads.1, bf16[4096,512]{1,0:T(8,128)(2,1)} %eig_in.1, bf16[16384,256]{1,0:T(8,128)(2,1)} %eig_out.1, bf16[256,4096]{1,0:T(8,128)(2,1)} %query_acts.1, ...), custom_call_target="tpu_custom_call" | custom-call | flops 9663676416 | bytes 31457280 | tf_op jit(solution)/shard_map/pallas_call | solution.py:348
  57.2 1.3 %copy.11 = f32[16,16]{1,0:T(8,128)} copy(f32[16,16]{1,0:T(8,128)} %shard_map.91) | data formatting | bytes 2048

commit v2 on v1

--- a/solution.py
+++ b/solution.py
@@ -24,20 +24,22 @@
 
 def kernel(
     sizes, len_ref, own_ref, acts, grads, eig_in, eig_out, query_acts, query_grads, eigenvalues, out_ref,
-    v_a, v_g, v_ei, v_eo, v_qa, v_qg,
-    acc_ti, acc_to, acc_qi, acc_qo,
-    send_ti, send_to, send_qi, send_qo,
-    got_ti, got_to, got_qi, got_qo,
-    tok_in, tok_out, que_in, que_out,
-    levels, doc_grad, que_grad, pair, placed, table,
+    v_a, v_g0, v_g1, v_ei, v_eo, v_qa, v_qg,
+    acc_ti, acc_to0, acc_to1, acc_qi, acc_qo,
+    send_ti, send_to0, send_to1, send_qi, send_qo,
+    got_ti, got_to0, got_to1, got_qi, got_qo,
+    tok_in, tok_out0, tok_out1, que_in, que_out,
+    levels, doc_grad, que_grad, pair, fold, placed, table,
     load_sem, x_send, x_recv, core_send, core_recv, z_send, z_recv, last_send, last_recv,
 ):
+    tok_out = (tok_out0, tok_out1)
     nz, nx, n_in, n_out, in_step, out_step, doc_count, capacity = sizes
     part, z, x, s = (lax.axis_index(name) for name in ("parts", "dp", "tensor", "seq"))
     n_all = nz * nx * 2
     me = (z * nx + x) * 2 + s
     rows, wide = acc_ti.shape[1:]
-    ks = acc_to.shape[1]
+    ks = acc_to0.shape[1]
+    half = rows // 2
     q_rows = acc_qo.shape[0]
     q_each = q_rows // QTOK
     q_all = nz * q_each
@@ -49,26 +51,28 @@
         src, dst = {
             "eo": lambda: (eig_out.at[pl.ds(c * out_step, out_step), :], v_eo.at[c]),
             "qg": lambda: (query_grads.at[:, pl.ds(c * out_step, out_step)], v_qg.at[c]),
-            "g": lambda: (grads.at[:, pl.ds(c * out_step, out_step)], v_g.at[c]),
+            "g0": lambda: (grads.at[pl.ds(0, half), pl.ds(c * out_step, out_step)], v_g0.at[c]),
+            "g1": lambda: (grads.at[pl.ds(half, half), pl.ds(c * out_step, out_step)], v_g1.at[c]),
             "ei": lambda: (eig_in.at[pl.ds(c * in_step, in_step), :], v_ei.at[c]),
             "qa": lambda: (query_acts.at[:, pl.ds(c * in_step, in_step)], v_qa.at[c]),
             "a": lambda: (acts.at[:, pl.ds(c * in_step, in_step)], v_a.at[c]),
         }[kind]()
-        row = ("eo", "qg", "g", "ei", "qa", "a").index(kind)
+        row = ("eo", "qg", "g0", "g1", "ei", "qa", "a").index(kind)
         return pltpu.make_async_copy(src, dst, load_sem.at[row, c])
 
+    for c in range(n_in):
+        load("ei", c).start()
+        load("qa", c).start()
     for c in range(n_out):
         load("eo", c).start()
         load("qg", c).start()
     for c in range(n_in):
-        load("ei", c).start()
-        load("qa", c).start()
-    for c in range(n_out):
-        load("g", c).start()
-    for c in range(n_in):
         load("a", c).start()
+    for kind in ("g0", "g1"):
+        for c in range(n_out):
+            load(kind, c).start()
     own_level = pltpu.make_async_copy(
-        eigenvalues.at[:, pl.ds(pl.multiple_of(x * wide, LANES), wide)], levels.at[x], load_sem.at[6, 0]
+        eigenvalues.at[:, pl.ds(pl.multiple_of(x * wide, LANES), wide)], levels.at[x], load_sem.at[7, 0]
     )
     own_level.start()
 
@@ -89,9 +93,10 @@
             "qi": lambda: (send_qi.at[other], got_qi),
             "qo": lambda: (send_qo, got_qo),
             "ti": lambda: (send_ti.at[other], got_ti),
-            "to": lambda: (send_to, got_to),
+            "to0": lambda: (send_to0, got_to0),
+            "to1": lambda: (send_to1, got_to1),
         }[kind]()
-        row = ("ev", "qi", "qo", "ti", "to").index(kind)
+        row = ("ev", "qi", "qo", "ti", "to0", "to1").index(kind)
 
         def copy(slot):
             return pltpu.make_async_remote_copy(
@@ -115,9 +120,7 @@
             total = total + got[lax.rem(x + nx - r, nx)].astype(f32)
         return total
 
-    def rotate_out(kind, held, acc):
-        acc[...] = jnp.zeros_like(acc)
-
+    def rotate_out(kind, held, acc, first, last):
         def step(c, carry):
             if kind == "qg":
                 load("eo", c).wait()
@@ -125,7 +128,7 @@
             acc[...] += dot(held[c], v_eo[c])
             return carry
 
-        lax.fori_loop(0, n_out, step, 0)
+        lax.fori_loop(first, last, step, 0)
 
     def rotate_in(kind, held, acc):
         acc[...] = jnp.zeros_like(acc)
@@ -140,19 +143,6 @@
 
         lax.fori_loop(0, n_in, step, 0)
 
-    rotate_out("qg", v_qg, acc_qo)
-    send_qo[...] = acc_qo[...].astype(bf16)
-    pl.semaphore_wait(barrier, n_all - 1)
-    start_x("ev")
-    start_x("qo")
-    rotate_in("qa", v_qa, acc_qi)
-    send_qi[...] = acc_qi[...].astype(bf16)
-    start_x("qi")
-
-    rotate_out("g", v_g, acc_to)
-    send_to[...] = acc_to[...].astype(bf16)
-    start_x("to")
-
     def along_z(kind, r, arriving=False):
         ref = que_out if kind == 0 else que_in
         other = lax.rem(z + r, nz)
@@ -166,106 +156,146 @@
 
         return copy(back if arriving else z)
 
-    wait_x("qo")
-    que_out[z] = summed(acc_qo[...], got_qo).T.astype(bf16)
+    def start_z(kind):
+        def one(r, carry):
+            along_z(kind, r).start()
+            return carry
+
+        lax.fori_loop(1, nz, one, 0)
+
+    acc_qo[...] = jnp.zeros_like(acc_qo)
+    acc_to0[...] = jnp.zeros_like(acc_to0)
+    acc_to1[...] = jnp.zeros_like(acc_to1)
+    placed[...] = jnp.zeros_like(placed)
+    rotate_in("qa", v_qa, acc_qi)
+    send_qi[...] = acc_qi[...].astype(bf16)
+    pl.semaphore_wait(barrier, n_all - 1)
+    start_x("qi")
+    rotate_out("qg", v_qg, acc_qo, 0, n_out // 2)
     wait_x("qi")
     que_in[z] = summed(acc_qi[x], got_qi).astype(bf16)
-
-    def start_z(r, carry):
-        along_z(0, r).start()
-        along_z(1, r).start()
-        return carry
-
-    lax.fori_loop(1, nz, start_z, 0)
+    start_z(1)
+    rotate_out("qg", v_qg, acc_qo, n_out // 2, n_out)
+    send_qo[...] = acc_qo[...].astype(bf16)
+    start_x("qo")
+    start_x("ev")
 
     rotate_in("a", v_a, acc_ti)
     send_ti[...] = acc_ti[...].astype(bf16)
     start_x("ti")
+    rotate_out("g0", v_g0, acc_to0, 0, n_out // 2)
+    wait_x("qo")
+    que_out[z] = summed(acc_qo[...], got_qo).T.astype(bf16)
+    start_z(0)
+    rotate_out("g0", v_g0, acc_to0, n_out // 2, n_out)
+    send_to0[...] = acc_to0[...].astype(bf16)
+    start_x("to0")
+
+    def to_core(kind, slot):
+        ref = (tok_out0.at[slot], tok_out1.at[slot], tok_in.at[slot])[kind]
+        return pltpu.make_async_remote_copy(
+            src_ref=ref, dst_ref=ref, send_sem=core_send.at[kind], recv_sem=core_recv.at[kind],
+            device_id=(part, z, x, 1 - s), device_id_type=MESH,
+        )
+
+    rotate_out("g1", v_g1, acc_to1, 0, n_out)
+    send_to1[...] = acc_to1[...].astype(bf16)
+    start_x("to1")
+    wait_x("ti")
+    tok_in[s] = summed(acc_ti[x], got_ti).astype(bf16)
+    to_core(2, s).start()
+    wait_x("to0")
+    tok_out0[s] = summed(acc_to0[...], got_to0).T.astype(bf16)
+    to_core(0, s).start()
 
     own_level.wait()
     wait_x("ev")
     levels[...] = 1.0 / (levels[...] + damping)
+    q_batch = min(4, q_each)
 
     def damp(zb):
         lane = lax.broadcasted_iota(jnp.int32, (1, q_rows), 1)
         scale = levels[...].reshape(ks, wide)
-
-        def one(k, carry):
-            keep = ((lane >= k * QTOK) & (lane < (k + 1) * QTOK)).astype(f32).astype(bf16)
-            outer = dot(que_out[zb] * keep, que_in[zb])
-            que_grad[:, zb * q_each + k] = (outer * scale).astype(bf16).reshape(ks // GROUP, GROUP, wide)
-            return carry
-
-        lax.fori_loop(0, q_each, one, 0)
+        for k0 in range(0, q_each, q_batch):
+            stack = []
+            for k in range(k0, k0 + q_batch):
+                keep = ((lane >= k * QTOK) & (lane < (k + 1) * QTOK)).astype(f32).astype(bf16)
+                stack.append(que_out[zb] * keep)
+            outer = dot(jnp.concatenate(stack, axis=0), que_in[zb])
+            for i in range(q_batch):
+                block = (outer[i * ks:(i + 1) * ks] * scale).astype(bf16)
+                que_grad[:, zb * q_each + k0 + i] = block.reshape(ks // GROUP, GROUP, wide)
 
     damp(z)
-
-    def to_core(kind, slot):
-        ref = tok_out if kind == 0 else tok_in
-        return pltpu.make_async_remote_copy(
-            src_ref=ref.at[slot], dst_ref=ref.at[slot], send_sem=core_send.at[kind], recv_sem=core_recv.at[kind],
-            device_id=(part, z, x, 1 - s), device_id_type=MESH,
-        )
-
-    wait_x("to")
-    tok_out[s] = summed(acc_to[...], got_to).T.astype(bf16)
-    to_core(0, s).start()
-    wait_x("ti")
-    tok_in[s] = summed(acc_ti[x], got_ti).astype(bf16)
+    wait_x("to1")
+    tok_out1[s] = summed(acc_to1[...], got_to1).T.astype(bf16)
     to_core(1, s).start()
-    to_core(0, 1 - s).wait_recv()
-    to_core(1, 1 - s).wait_recv()
-
-    def document(d, begin):
-        end = begin + len_ref[0, d]
-        total = None
-        for half in range(2):
-            at = lax.broadcasted_iota(jnp.int32, (1, rows), 1) + half * rows
-            keep = ((at >= begin) & (at < end)).astype(f32).astype(bf16)
-            term = dot(tok_out[half] * keep, tok_in[half])
-            total = term if total is None else total + term
-        doc_grad[:, d] = total.astype(bf16).reshape(ks // GROUP, GROUP, wide)
-        return end
-
-    lax.fori_loop(0, doc_count, document, jnp.int32(0))
-
-    def damp_far(r, carry):
-        along_z(0, r, True).wait_recv()
-        along_z(1, r, True).wait_recv()
-        damp(lax.rem(z + nz - r, nz))
-        return carry
-
-    lax.fori_loop(1, nz, damp_far, 0)
-
-    pair[...] = jnp.zeros_like(pair)
-
-    def pairs(g, carry):
-        left = doc_grad[g].reshape(doc_count * GROUP, wide)
-        right = que_grad[g].reshape(q_all * GROUP, wide)
-        pair[...] += dot(left, right, ((1,), (1,)))
-        return carry
-
-    lax.fori_loop(0, ks // GROUP, pairs, 0)
-    row = lax.broadcasted_iota(jnp.int32, pair.shape, 0)
-    col = lax.broadcasted_iota(jnp.int32, pair.shape, 1)
-    same = jnp.where(lax.rem(row, GROUP) == lax.rem(col, GROUP), pair[...], 0.0)
-    by_doc = jnp.sum(same.reshape(doc_count, GROUP, q_all * GROUP), axis=1)
-    fold_row = lax.broadcasted_iota(jnp.int32, (q_all * GROUP, LANES), 0)
-    fold_col = lax.broadcasted_iota(jnp.int32, (q_all * GROUP, LANES), 1)
-    fold = (lax.div(fold_row, GROUP) == fold_col).astype(f32)
-    highest = lax.Precision.HIGHEST
-    scores = dot(by_doc, fold, precision=highest)
-
-    slot_row = lax.broadcasted_iota(jnp.int32, (nz * PAD, doc_count), 0)
-    slot_col = lax.broadcasted_iota(jnp.int32, (nz * PAD, doc_count), 1)
-    placing = jnp.zeros((nz * PAD, doc_count), f32)
+
+    fold_row = lax.broadcasted_iota(jnp.int32, fold.shape, 0)
+    fold_col = lax.broadcasted_iota(jnp.int32, fold.shape, 1)
+    folding = jnp.zeros(fold.shape, f32)
     for d in range(doc_count):
         owner = own_ref[0, d]
         slot = jnp.int32(0)
         for e in range(d):
             slot = slot + jnp.where(own_ref[0, e] == owner, 1, 0)
-        placing = jnp.where((slot_row == owner * PAD + slot) & (slot_col == d), 1.0, placing)
-    placed[...] = dot(placing, scores, precision=highest).reshape(nz, PAD, LANES)
+        here = (fold_row == owner * PAD + slot) & (fold_col >= d * GROUP) & (fold_col < (d + 1) * GROUP)
+        folding = jnp.where(here, 1.0, folding)
+    fold[...] = folding
+
+    for kind in range(3):
+        to_core(kind, 1 - s).wait_recv()
+
+    batch = min(4, doc_count)
+
+    def documents(k, begin):
+        ends = [begin]
+        for i in range(batch):
+            ends.append(ends[-1] + len_ref[0, k * batch + i])
+        total = None
+        for side in range(2):
+            for h in range(2):
+                at = lax.broadcasted_iota(jnp.int32, (1, half), 1) + (side * rows + h * half)
+                stack = []
+                for i in range(batch):
+                    keep = ((at >= ends[i]) & (at < ends[i + 1])).astype(f32).astype(bf16)
+                    stack.append(tok_out[h][side] * keep)
+                term = dot(jnp.concatenate(stack, axis=0), tok_in[side, h * half:(h + 1) * half, :])
+                total = term if total is None else total + term
+        for i in range(batch):
+            block = total[i * ks:(i + 1) * ks].astype(bf16)
+            doc_grad[:, k * batch + i] = block.reshape(ks // GROUP, GROUP, wide)
+        return ends[-1]
+
+    lax.fori_loop(0, doc_count // batch, documents, jnp.int32(0))
+
+    def damp_far(r, carry):
+        along_z(0, r, True).wait_recv()
+        along_z(1, r, True).wait_recv()
+        damp(lax.rem(z + nz - r, nz))
+        return carry
+
+    lax.fori_loop(1, nz, damp_far, 0)
+
+    pair[...] = jnp.zeros_like(pair)
+
+    def pairs(g, carry):
+        total = None
+        for i in range(4):
+            left = que_grad[g * 4 + i].reshape(q_all * GROUP, wide)
+            right = doc_grad[g * 4 + i].reshape(doc_count * GROUP, wide)
+            term = dot(left, right, ((1,), (1,)))
+            total = term if total is None else total + term
+        pair[...] += total
+        return carry
+
+    lax.fori_loop(0, ks // GROUP // 4, pairs, 0)
+    row = lax.broadcasted_iota(jnp.int32, pair.shape, 0)
+    col = lax.broadcasted_iota(jnp.int32, pair.shape, 1)
+    same = jnp.where(lax.rem(row, GROUP) == lax.rem(col, GROUP), pair[...], 0.0)
+    by_query = jnp.sum(same.reshape(q_all, GROUP, doc_count * GROUP), axis=1)
+    highest = lax.Precision.HIGHEST
+    placed[:, :, 0:q_all] = dot(fold[...], by_query, ((1,), (1,)), highest).reshape(nz, PAD, q_all)
 
     def to_owner(r):
         oz, ox, os = place(lax.rem(me + r, n_all))
@@ -288,11 +318,11 @@
     lax.fori_loop(1, n_all, start_last, 0)
     table[x * 2 + s, z] = placed[z]
 
-    for kind in ("ev", "qi", "qo", "ti", "to"):
+    for kind in ("ev", "qi", "qo", "ti", "to0", "to1"):
         for r in range(1, nx):
             along_x(kind, r).wait_send()
-    to_core(0, s).wait_send()
-    to_core(1, s).wait_send()
+    for kind in range(3):
+        to_core(kind, s).wait_send()
 
     def sent_z(r, carry):
         along_z(0, r).wait_send()
@@ -352,38 +382,44 @@
         out_specs=pl.BlockSpec(memory_space=pltpu.VMEM),
         scratch_shapes=[
             pltpu.VMEM((n_in, rows, in_step), bf16),
-            pltpu.VMEM((n_out, rows, out_step), bf16),
+            pltpu.VMEM((n_out, rows // 2, out_step), bf16),
+            pltpu.VMEM((n_out, rows // 2, out_step), bf16),
             pltpu.VMEM((n_in, in_step, ka), bf16),
             pltpu.VMEM((n_out, out_step, ks), bf16),
             pltpu.VMEM((n_in, q_rows, in_step), bf16),
             pltpu.VMEM((n_out, q_rows, out_step), bf16),
             pltpu.VMEM((nx, rows, wide), f32),
-            pltpu.VMEM((rows, ks), f32),
+            pltpu.VMEM((rows // 2, ks), f32),
+            pltpu.VMEM((rows // 2, ks), f32),
             pltpu.VMEM((nx, q_rows, wide), f32),
             pltpu.VMEM((q_rows, ks), f32),
             pltpu.VMEM((nx, rows, wide), bf16),
-            pltpu.VMEM((rows, ks), bf16),
+            pltpu.VMEM((rows // 2, ks), bf16),
+            pltpu.VMEM((rows // 2, ks), bf16),
             pltpu.VMEM((nx, q_rows, wide), bf16),
             pltpu.VMEM((q_rows, ks), bf16),
             pltpu.VMEM((nx, rows, wide), bf16),
-            pltpu.VMEM((nx, rows, ks), bf16),
+            pltpu.VMEM((nx, rows // 2, ks), bf16),
+            pltpu.VMEM((nx, rows // 2, ks), bf16),
             pltpu.VMEM((nx, q_rows, wide), bf16),
             pltpu.VMEM((nx, q_rows, ks), bf16),
             pltpu.VMEM((2, rows, wide), bf16),
-            pltpu.VMEM((2, ks, rows), bf16),
+            pltpu.VMEM((2, ks, rows // 2), bf16),
+            pltpu.VMEM((2, ks, rows // 2), bf16),
             pltpu.VMEM((nz, q_rows, wide), bf16),
             pltpu.VMEM((nz, ks, q_rows), bf16),
             pltpu.VMEM((nx, ks // nx, wide), f32),
             pltpu.VMEM((ks // GROUP, doc_count, GROUP, wide), bf16),
             pltpu.VMEM((ks // GROUP, q_all, GROUP, wide), bf16),
-            pltpu.VMEM((doc_count * GROUP, q_all * GROUP), f32),
+            pltpu.VMEM((q_all * GROUP, doc_count * GROUP), f32),
+            pltpu.VMEM((nz * PAD, doc_count * GROUP), f32),
             pltpu.VMEM((nz, PAD, LANES), f32),
             pltpu.VMEM((nx * 2, nz, PAD, LANES), f32),
-            dma((7, max(n_in, n_out))),
-            dma((5, nx)),
-            dma((5, nx)),
-            dma((2,)),
-            dma((2,)),
+            dma((8, max(n_in, n_out))),
+            dma((6, nx)),
+            dma((6, nx)),
+            dma((3,)),
+            dma((3,)),
             dma((2, nz)),
             dma((2, nz)),
             dma((n_all,)),

time: 58.7 us -> 46.9 us (0.80)
  Pallas kernels: 57.2 us -> 45.4 us
    pallas_call x1, Pallas kernels: 57.2 us -> 45.4 us  [per_device(): pl.pallas_call(functools.partial(kernel, sizes), out_shape=jax.ShapeDtype...]
where the time goes in v2:
time: 46.9 us; the launch traced here: 46.7 us
  Pallas kernels  45.4 us (97%)
  local copies, waits for them, and re-layouts  1.3 us (3%)
    pallas_call x1, Pallas kernels, per_device(): pl.pallas_call(functools.partial(kernel, sizes), out_shape=jax.ShapeDtype...  45.4 us
    unnamed x1, local copies, waits for them, and re-layouts  1.3 us

profile of v2, /device:TPU:0, one launch (start us, length us, event | category | flops | bytes accessed | tf_op | source)
XLA Modules:
  0.0 46.7 jit_solution(7466507072401617227)
XLA Ops:
  0.0 45.4 %shard_map.91 = f32[16,16]{1,0:T(8,128)} custom-call(s32[1,16]{1,0:T(1,128)} %len_ref.1, s32[1,16]{1,0:T(1,128)} %bitcast.1, bf16[512,4096]{1,0:T(8,128)(2,1)} %acts.1, bf16[512,16384]{1,0:T(8,128)(2,1)} %grads.1, bf16[4096,512]{1,0:T(8,128)(2,1)} %eig_in.1, bf16[16384,256]{1,0:T(8,128)(2,1)} %eig_out.1, bf16[256,4096]{1,0:T(8,128)(2,1)} %query_acts.1, ...), custom_call_target="tpu_custom_call" | custom-call | flops 9663676416 | bytes 31457280 | tf_op jit(solution)/shard_map/pallas_call | solution.py:378
  45.4 1.3 %copy.11 = f32[16,16]{1,0:T(8,128)} copy(f32[16,16]{1,0:T(8,128)} %shard_map.91) | data formatting | bytes 2048

commit v3 on v2

--- a/solution.py
+++ b/solution.py
@@ -167,9 +167,10 @@
     acc_to0[...] = jnp.zeros_like(acc_to0)
     acc_to1[...] = jnp.zeros_like(acc_to1)
     placed[...] = jnp.zeros_like(placed)
+    pl.semaphore_wait(barrier, n_all - 1)
+    start_x("ev")
     rotate_in("qa", v_qa, acc_qi)
     send_qi[...] = acc_qi[...].astype(bf16)
-    pl.semaphore_wait(barrier, n_all - 1)
     start_x("qi")
     rotate_out("qg", v_qg, acc_qo, 0, n_out // 2)
     wait_x("qi")
@@ -178,7 +179,6 @@
     rotate_out("qg", v_qg, acc_qo, n_out // 2, n_out)
     send_qo[...] = acc_qo[...].astype(bf16)
     start_x("qo")
-    start_x("ev")
 
     rotate_in("a", v_a, acc_ti)
     send_ti[...] = acc_ti[...].astype(bf16)
@@ -242,6 +242,14 @@
         here = (fold_row == owner * PAD + slot) & (fold_col >= d * GROUP) & (fold_col < (d + 1) * GROUP)
         folding = jnp.where(here, 1.0, folding)
     fold[...] = folding
+
+    def damp_far(r, carry):
+        along_z(0, r, True).wait_recv()
+        along_z(1, r, True).wait_recv()
+        damp(lax.rem(z + nz - r, nz))
+        return carry
+
+    lax.fori_loop(1, nz, damp_far, 0)
 
     for kind in range(3):
         to_core(kind, 1 - s).wait_recv()
@@ -268,14 +276,6 @@
         return ends[-1]
 
     lax.fori_loop(0, doc_count // batch, documents, jnp.int32(0))
-
-    def damp_far(r, carry):
-        along_z(0, r, True).wait_recv()
-        along_z(1, r, True).wait_recv()
-        damp(lax.rem(z + nz - r, nz))
-        return carry
-
-    lax.fori_loop(1, nz, damp_far, 0)
 
     pair[...] = jnp.zeros_like(pair)
 

time: 46.9 us -> 52.2 us (1.11)
  Pallas kernels: 45.4 us -> 50.7 us
    pallas_call x1, Pallas kernels: 45.4 us -> 50.7 us  [per_device(): pl.pallas_call(functools.partial(kernel, sizes), out_shape=jax.ShapeDtype...]
where the time goes in v3:
time: 52.2 us; the launch traced here: 52 us
  Pallas kernels  50.7 us (97%)
  local copies, waits for them, and re-layouts  1.3 us (2%)
    pallas_call x1, Pallas kernels, per_device(): pl.pallas_call(functools.partial(kernel, sizes), out_shape=jax.ShapeDtype...  50.7 us
    unnamed x1, local copies, waits for them, and re-layouts  1.3 us

profile of v3, /device:TPU:0, one launch (start us, length us, event | category | flops | bytes accessed | tf_op | source)
XLA Modules:
  0.0 52.0 jit_solution(7281394476893333160)
XLA Ops:
  0.0 50.7 %shard_map.91 = f32[16,16]{1,0:T(8,128)} custom-call(s32[1,16]{1,0:T(1,128)} %len_ref.1, s32[1,16]{1,0:T(1,128)} %bitcast.1, bf16[512,4096]{1,0:T(8,128)(2,1)} %acts.1, bf16[512,16384]{1,0:T(8,128)(2,1)} %grads.1, bf16[4096,512]{1,0:T(8,128)(2,1)} %eig_in.1, bf16[16384,256]{1,0:T(8,128)(2,1)} %eig_out.1, bf16[256,4096]{1,0:T(8,128)(2,1)} %query_acts.1, ...), custom_call_target="tpu_custom_call" | custom-call | flops 9663676416 | bytes 31457280 | tf_op jit(solution)/shard_map/pallas_call | solution.py:378
  50.7 1.3 %copy.11 = f32[16,16]{1,0:T(8,128)} copy(f32[16,16]{1,0:T(8,128)} %shard_map.91) | data formatting | bytes 2048
